TPU v7x, 128 devices: a whole 4x4x4 slice. The times are simulated.
128 devices in a mesh: row: 4 (over y), col: 4 (over x_lo, core), freq: 8 (over z, x_hi).
Axes of the slice: x: 4 (x_hi: 2, x_lo: 2; x = x_hi * 2 + x_lo), y: 4, z: 4, core: 2. Of those that a mesh axis runs over, the one named last changes fastest.
Arguments:
- traces: bfloat16 [1280, 224, 512], P(('row', 'col'), 'freq'), may hold values from -6 to 6
- window_mask: int32 [1280, 224], P(('row', 'col'), 'freq'), may hold values 0 or 1
Outputs:
- cross_spectra: bfloat16 [2, 256, 1280, 1280], P(None, 'freq', 'row', 'col')
All inputs are finite; a program needn't handle non-finite values. No bound on the sum of `window_mask` on one device may be relied on, other than what follows from the above.
Results may differ from a plain program's by a relative error of at most 0.0065.
Values may be sent and summed in bfloat16 or wider, within the bound.
A program may use at most 192 MiB of HBM per device.

v0:
```python
import math
import jax
import jax.numpy as jnp
from jax import lax
from jax.sharding import PartitionSpec as P

SAMPLES = 512
BINS = 256
epsilon = 1e-06


def dft_table():
    sample_idx = jnp.arange(SAMPLES, dtype=jnp.int32)
    bin_idx = jnp.arange(BINS, dtype=jnp.int32)
    phase = bin_idx[:, None] * sample_idx[None, :] % SAMPLES
    angles = 2.0 * math.pi / SAMPLES * phase.astype(jnp.float32)
    taper = 0.5 - 0.5 * jnp.cos(2.0 * math.pi / SAMPLES * sample_idx.astype(jnp.float32))
    stacked = jnp.stack(
        [taper[None, :] * jnp.cos(angles), -taper[None, :] * jnp.sin(angles)], axis=1
    )
    return stacked.reshape(2 * BINS, SAMPLES).astype(jnp.bfloat16)


def shards(traces, window_mask):
    dft = dft_table()
    spectrum = jnp.einsum("kt,swt->skw", dft, traces, preferred_element_type=jnp.float32)
    energy = jnp.mean(spectrum * spectrum, axis=1)
    factor = window_mask.astype(jnp.float32) * lax.rsqrt(energy + epsilon)
    whitened = (spectrum * factor[:, None, :]).astype(jnp.bfloat16)
    regrouped = lax.all_to_all(whitened, "freq", split_axis=1, concat_axis=2, tiled=True)
    everyone = lax.all_gather(regrouped, ("row", "col"), axis=0, tiled=True)
    block_rows = regrouped.shape[0] * lax.axis_size("col")
    row_stations = lax.dynamic_slice_in_dim(
        everyone, lax.axis_index("row") * block_rows, block_rows, 0
    )
    col_stations = lax.dynamic_slice_in_dim(
        everyone, lax.axis_index("col") * block_rows, block_rows, 0
    )
    windows_all = regrouped.shape[2]
    bins_here = regrouped.shape[1] // 2
    left_side = row_stations.reshape(row_stations.shape[0], bins_here, 2, windows_all)
    right_side = col_stations.reshape(col_stations.shape[0], bins_here, 2, windows_all)
    products = jnp.einsum(
        "ifcw,jfdw->fcdij", left_side, right_side, preferred_element_type=jnp.float32
    )
    norm_scale = 1.0 / math.sqrt(windows_all)
    real_part = (products[:, 0, 0] + products[:, 1, 1]) * norm_scale
    imag_part = (products[:, 1, 0] - products[:, 0, 1]) * norm_scale
    return jnp.stack([real_part, imag_part]).astype(jnp.bfloat16)


def solution(mesh):
    placed = (P(("row", "col"), "freq", None), P(("row", "col"), "freq"))
    return jax.shard_map(
        shards, mesh=mesh, in_specs=placed, out_specs=P(None, "freq", "row", "col"), check_vma=False
    )
```

profile of v0, /device:TPU:9, one launch (start us, length us, event | category | flops | bytes accessed | tf_op | source)
XLA Modules:
  0.0 428.0 jit_solution(7062251369111572887)
XLA Ops:
  6.5 0.0 copy-start
  6.5 0.0 copy-start.2
  6.5 0.0 all-gather.2.cloned.1.call-start
  6.6 2.2 multiply_convert_fusion.1
  8.9 0.1 pad_maximum_fusion.1
  8.9 0.5 copy.34
  9.5 0.2 reshape.179
  9.7 0.0 copy-done
  9.7 1.5 multiply_reduce_fusion
  11.2 0.0 copy-done.2
  11.2 0.4 fusion.7
  11.6 6.7 %copy.35 = bf16[80,512,28]{0,2,1:T(8,128)(2,1)} copy(bf16[80,512,28]{1,0,2:T(8,128)(2,1)S(1)} %fusion.7) | data formatting | bytes 4587520 | tf_op jit(solution)/shard_map/convert_element_type | solution.py:29
  18.3 57.5 %all_to_all.18 = bf16[80,512,28]{0,2,1:T(8,128)(2,1)S(1)} all-to-all(bf16[80,512,28]{0,2,1:T(8,128)(2,1)} %copy.35), channel_id=1, replica_groups=mesh['row'=4,'col'=4,'freq'=8] {'freq'}, dimensions={1} | all-to-all | bytes 4587520 | tf_op jit(solution)/shard_map/all_to_all | solution.py:30
  75.8 3.3 copy.37
  79.1 7.7 %copy.38 = bf16[80,64,224]{2,1,0:T(8,128)(2,1)} copy(bf16[80,64,224]{0,1,2:T(8,128)(2,1)} %bitcast.50) | data formatting | bytes 4587520 | tf_op jit(solution)/shard_map/all_to_all | solution.py:30
  86.7 0.0 all-gather.2.cloned.1.call-update
  86.7 209.4 %all-gather.2.cloned.1.call-done = bf16[1280,64,224]{2,1,0:T(8,128)(2,1)} async-done(((bf16[80,64,224]{2,1,0:T(8,128)(2,1)}), bf16[1280,64,224]{2,1,0:T(8,128)(2,1)}) %all-gather.2.cloned.1.call-update) | async-done | bytes 36700176 | tf_op jit(solution)/shard_map/all_gather | solution.py:31
  296.1 17.5 %constant_dynamic-slice_fusion = (bf16[320,64,224]{2,1,0:T(8,128)(2,1)}, bf16[320,64,224]{2,1,0:T(8,128)(2,1)}) fusion(bf16[1280,64,224]{2,1,0:T(8,128)(2,1)} %all-gather.2.cloned.1.call-done, s32[]{:T(128)S(6)} %select_n.28, s32[]{:T(128)S(6)} %select_n.27), kind=kLoop, calls=%fused_computation.30 | loop fusion | bytes 36700168 | tf_op jit(solution)/shard_map/dynamic_slice | solution.py:33
  313.7 13.9 %copy.40 = bf16[320,64,224]{2,0,1:T(8,128)(2,1)} copy(bf16[320,64,224]{2,1,0:T(8,128)(2,1)} %get-tuple-element.5) | data formatting | bytes 18350080 | tf_op jit(solution)/shard_map/dynamic_slice | solution.py:33
  327.6 14.2 %copy.39 = bf16[320,64,224]{2,0,1:T(8,128)(2,1)} copy(bf16[320,64,224]{2,1,0:T(8,128)(2,1)} %get-tuple-element.6) | data formatting | bytes 18350080 | tf_op jit(solution)/shard_map/dynamic_slice | solution.py:36
  341.8 29.1 %convolution_bitcast_fusion = f32[32,2,2,320,320]{3,4,1,2,0:T(8,128)} fusion(bf16[320,32,2,224,1]{3,0,4,2,1:T(8,128)(2,1)} %bitcast.48, bf16[320,32,2,224,1]{3,0,2,4,1:T(8,128)(2,1)} %bitcast.47), kind=kOutput, calls=%fused_computation | convolution fusion | flops 5872025600 | bytes 70778880 | tf_op jit(solution)/shard_map/ifcw,jfdw->fcdij/dot_general | solution.py:43
  370.9 10.9 %fusion.6 = bf16[1,32,320,320]{2,3,1,0:T(8,128)(2,1)S(1)} fusion(f32[32,2,2,320,320]{3,4,1,2,0:T(8,128)} %convolution_bitcast_fusion), kind=kLoop, calls=%fused_computation.11 | loop fusion | flops 9830400 | bytes 32768000 | tf_op jit(solution)/shard_map/mul | solution.py:48
  381.8 10.9 %fusion.5 = bf16[1,32,320,320]{2,3,1,0:T(8,128)(2,1)S(1)} fusion(f32[32,2,2,320,320]{3,4,1,2,0:T(8,128)} %convolution_bitcast_fusion), kind=kLoop, calls=%fused_computation.10 | loop fusion | flops 9830400 | bytes 32768000 | tf_op jit(solution)/shard_map/mul | solution.py:47
  392.7 0.0 copy-start.1
  392.7 7.5 %pad_maximum_fusion = bf16[2,32,320,320]{2,3,1,0:T(8,128)(2,1)} fusion(bf16[1,32,320,320]{2,3,1,0:T(8,128)(2,1)S(1)} %fusion.6, bf16[1,32,320,320]{2,3,1,0:T(8,128)(2,1)S(1)} %fusion.5), kind=kLoop, calls=%fused_computation.9 | loop fusion | flops 6553600 | bytes 26214400 | tf_op jit(solution)/shard_map/stack | solution.py:49
  400.2 20.9 %copy.44 = bf16[2,32,320,320]{3,2,1,0:T(8,128)(2,1)} copy(bf16[2,32,320,320]{2,3,1,0:T(8,128)(2,1)} %pad_maximum_fusion) | data formatting | bytes 26214400 | tf_op jit(solution)/shard_map/stack | solution.py:49
  421.1 0.0 copy-done.1
  (3 shorter events, 0.1 us)
Async XLA Ops:
  6.5 3.2 copy-start
  6.5 4.7 %copy-start.2 = (s32[80,28]{0,1:T(8,128)S(1)}, s32[80,28]{0,1:T(8,128)}, u32[]{:S(2)}) copy-start(s32[80,28]{0,1:T(8,128)} %param.3) | copy-start | bytes 26884
  6.5 289.6 %all-gather.2.cloned.1.call-start = ((), (), s32[]{:S(2)}) async-start(), calls=%async_computation.1 | async-start | bytes 44564480 | tf_op jit(solution)/shard_map/all_gather | solution.py:31
  392.7 28.4 %copy-start.1 = (bf16[80,28,512]{2,0,1:T(8,128)(2,1)S(1)}, bf16[80,28,512]{2,0,1:T(8,128)(2,1)}, u32[]{:S(2)}) copy-start(bf16[80,28,512]{2,0,1:T(8,128)(2,1)} %param.2) | copy-start | bytes 6881284
Sparse Core Ops, SparseCore 0:
  86.9 209.2 all-gather.1
where the time goes:
time: 429 us; the launch traced here: 428 us
  waiting for transfers between devices  209 us (49%)
  local copies, waits for them, and re-layouts  85 us (20%)
  blocking collectives  57.5 us (13%)
  other arithmetic  32.1 us (7%)
  matrix products  30.6 us (7%)
  between operations  13.5 us (3%)
    all_gather x1, waiting for transfers between devices, shards(): everyone = lax.all_gather(regrouped, ('row', 'col'), axis=0, tiled=True)  209 us
    all_to_all x1, blocking collectives, shards(): lax.all_to_all(whitened, 'freq', split_axis=1, concat_axis=2, tiled=True)  57.5 us
    dynamic_slice x2, local copies, waits for them, and re-layouts, shards(): lax.dynamic_slice_in_dim(everyone, lax.axis_index('row') * block_rows, bl...  31.4 us
    dot_general x1, matrix products, shards(): jnp.einsum('ifcw,jfdw->fcdij', left_side, right_side, preferred_element_t...  29.1 us
    another operation x1, local copies, waits for them, and re-layouts, shards(): return jnp.stack([real_part, imag_part]).astype(jnp.bfloat16)  20.9 us
    dynamic_slice x1, local copies, waits for them, and re-layouts, shards(): lax.dynamic_slice_in_dim(everyone, lax.axis_index('col') * block_rows, bl...  14.2 us
    mul x1, other arithmetic, shards(): real_part = (products[:, 0, 0] + products[:, 1, 1]) * norm_scale  10.9 us
    all_to_all x2, local copies, waits for them, and re-layouts, shards(): lax.all_to_all(whitened, 'freq', split_axis=1, concat_axis=2, tiled=True)  10.9 us
  transfers between devices with their start and end apart: 1, of which 1 were waited for; matrix products, arithmetic and copies ran while one was open for 0% of the time, Pallas kernels for 0%

commit v1 on v0

--- a/solution.py
+++ b/solution.py
@@ -1,3 +1,4 @@
+import functools
 import math
 import jax
 import jax.numpy as jnp
@@ -7,6 +8,19 @@
 SAMPLES = 512
 BINS = 256
 epsilon = 1e-06
+
+
+def fix_the_lines(inp, ndim_at, d_out):
+    now = lax.all_to_all(
+        jnp.stack(jnp.split(inp, lax.axis_size("freq"), ndim_at), axis=0),
+        concat_axis=0,
+        split_axis=0,
+        axis_name="freq",
+    )
+    return jnp.concatenate(now, d_out)
+
+
+guide_weights = functools.partial(fix_the_lines, ndim_at=1, d_out=2)
 
 
 def dft_table():
@@ -27,7 +41,7 @@
     energy = jnp.mean(spectrum * spectrum, axis=1)
     factor = window_mask.astype(jnp.float32) * lax.rsqrt(energy + epsilon)
     whitened = (spectrum * factor[:, None, :]).astype(jnp.bfloat16)
-    regrouped = lax.all_to_all(whitened, "freq", split_axis=1, concat_axis=2, tiled=True)
+    regrouped = guide_weights(whitened)
     everyone = lax.all_gather(regrouped, ("row", "col"), axis=0, tiled=True)
     block_rows = regrouped.shape[0] * lax.axis_size("col")
     row_stations = lax.dynamic_slice_in_dim(

time: 429 us -> 397 us (0.925)
  local copies, waits for them, and re-layouts: 85 us -> 58.3 us
  blocking collectives: 57.5 us -> 52 us
    dynamic_slice x2 -> x1, local copies, waits for them, and re-layouts: 31.4 us -> 16.7 us  [shards(): lax.dynamic_slice_in_dim(everyone, lax.axis_index('row') * block_rows, bl...]
    dynamic_slice x1 -> x0, local copies, waits for them, and re-layouts: 14.2 us -> none  [shards(): lax.dynamic_slice_in_dim(everyone, lax.axis_index('col') * block_rows, bl...]
    all_to_all x2 -> x0, local copies, waits for them, and re-layouts: 10.9 us -> none  [shards(): lax.all_to_all(whitened, 'freq', split_axis=1, concat_axis=2, tiled=True)]
    another operation x0 -> x2, local copies, waits for them, and re-layouts: none -> 7.4 us  [fix_the_lines(): jnp.stack(jnp.split(inp, lax.axis_size('freq'), ndim_at), axis=0)]
    unnamed x6 -> x13, local copies, waits for them, and re-layouts: 0.01 us -> 6.75 us
    convert_element_type x1 -> x0, local copies, waits for them, and re-layouts: 6.7 us -> none  [shards(): whitened = (spectrum * factor[:, None, :]).astype(jnp.bfloat16)]
    reshape x0 -> x1, local copies, waits for them, and re-layouts: none -> 5.64 us  [fix_the_lines(): return jnp.concatenate(now, d_out)]
    all_to_all x1, blocking collectives: 57.5 us -> 52 us  [fix_the_lines(): lax.all_to_all(jnp.stack(jnp.split(inp, lax.axis_size('freq'), ndim_at),...]
where the time goes in v1:
time: 397 us; the launch traced here: 396 us
  waiting for transfers between devices  209 us (53%)
  local copies, waits for them, and re-layouts  58.3 us (15%)
  blocking collectives  52 us (13%)
  other arithmetic  32.1 us (8%)
  matrix products  30.6 us (8%)
  between operations  13.5 us (3%)
    all_gather x1, waiting for transfers between devices, shards(): everyone = lax.all_gather(regrouped, ('row', 'col'), axis=0, tiled=True)  209 us
    all_to_all x1, blocking collectives, fix_the_lines(): lax.all_to_all(jnp.stack(jnp.split(inp, lax.axis_size('freq'), ndim_at),...  52 us
    dot_general x1, matrix products, shards(): jnp.einsum('ifcw,jfdw->fcdij', left_side, right_side, preferred_element_t...  29.1 us
    another operation x1, local copies, waits for them, and re-layouts, shards(): return jnp.stack([real_part, imag_part]).astype(jnp.bfloat16)  21.1 us
    dynamic_slice x1, local copies, waits for them, and re-layouts, shards(): lax.dynamic_slice_in_dim(everyone, lax.axis_index('row') * block_rows, bl...  16.7 us
    mul x1, other arithmetic, shards(): real_part = (products[:, 0, 0] + products[:, 1, 1]) * norm_scale  10.9 us
    mul x1, other arithmetic, shards(): imag_part = (products[:, 1, 0] - products[:, 0, 1]) * norm_scale  10.9 us
  transfers between devices with their start and end apart: 1, of which 1 were waited for; matrix products, arithmetic and copies ran while one was open for 0% of the time, Pallas kernels for 0%

profile of v1, /device:TPU:9, one launch (start us, length us, event | category | flops | bytes accessed | tf_op | source)
XLA Modules:
  0.0 395.7 jit_solution(9253051865816672454)
XLA Ops:
  6.5 0.0 copy-start
  6.5 0.0 all-gather.2.cloned.1.call-start
  6.6 2.2 multiply_convert_fusion.1
  8.9 0.1 pad_maximum_fusion.1
  8.9 0.5 copy.21
  9.5 0.2 reshape.187
  9.7 0.0 copy-done
  9.7 0.0 copy-start.2
  9.7 1.5 multiply_reduce_fusion
  11.2 0.0 copy-done.2
  11.2 0.4 fusion.7
  11.6 0.9 fusion.15
  12.5 1.0 fusion.14
  13.6 0.9 fusion.13
  14.5 1.0 fusion.12
  15.5 0.9 fusion.11
  16.4 1.0 fusion.10
  17.4 0.9 fusion.9
  18.4 1.0 fusion.8
  19.4 6.4 %copy.22 = bf16[8,80,64,28]{1,2,3,0:T(8,128)(2,1)} copy(bf16[8,80,64,28]{2,1,3,0:T(8,128)(2,1)} %fusion.8) | data formatting | bytes 4587520 | tf_op jit(solution)/shard_map/stack | solution.py:15
  25.8 52.0 %all_to_all.5 = bf16[8,80,64,28]{1,2,3,0:T(8,128)(2,1)} all-to-all(bf16[8,80,64,28]{1,2,3,0:T(8,128)(2,1)} %copy.22), channel_id=1, replica_groups=mesh['row'=4,'col'=4,'freq'=8] {'freq'}, dimensions={0} | all-to-all | bytes 4587520 | tf_op jit(solution)/shard_map/all_to_all | solution.py:14
  77.7 5.6 %copy.23 = bf16[80,64,224]{2,0,1:T(8,128)(2,1)} copy(bf16[80,64,224]{0,1,2:T(8,128)(2,1)} %bitcast.79) | data formatting | bytes 4587520 | tf_op jit(solution)/shard_map/reshape | solution.py:20
  83.4 0.0 all-gather.2.cloned.1.call-update
  83.4 209.3 %all-gather.2.cloned.1.call-done = bf16[1280,64,224]{2,0,1:T(8,128)(2,1)} async-done(((bf16[80,64,224]{2,0,1:T(8,128)(2,1)}), bf16[1280,64,224]{2,0,1:T(8,128)(2,1)}) %all-gather.2.cloned.1.call-update) | async-done | bytes 36700176 | tf_op jit(solution)/shard_map/all_gather | solution.py:45
  292.7 16.7 %constant_dynamic-slice_fusion = (bf16[320,64,224]{2,0,1:T(8,128)(2,1)}, bf16[320,64,224]{2,0,1:T(8,128)(2,1)}) fusion(bf16[1280,64,224]{2,0,1:T(8,128)(2,1)} %all-gather.2.cloned.1.call-done, s32[]{:T(128)S(6)} %select_n.28, s32[]{:T(128)S(6)} %select_n.27), kind=kLoop, calls=%fused_computation.46 | loop fusion | bytes 36700168 | tf_op jit(solution)/shard_map/dynamic_slice | solution.py:47
  309.4 29.1 %convolution_bitcast_fusion = f32[32,2,2,320,320]{3,4,1,2,0:T(8,128)} fusion(bf16[320,32,2,224,1]{3,0,4,2,1:T(8,128)(2,1)} %bitcast.78, bf16[320,32,2,224,1]{3,0,2,4,1:T(8,128)(2,1)} %bitcast.77), kind=kOutput, calls=%fused_computation | convolution fusion | flops 5872025600 | bytes 70778880 | tf_op jit(solution)/shard_map/ifcw,jfdw->fcdij/dot_general | solution.py:57
  338.5 10.9 %fusion.6 = bf16[1,32,320,320]{2,3,1,0:T(8,128)(2,1)S(1)} fusion(f32[32,2,2,320,320]{3,4,1,2,0:T(8,128)} %convolution_bitcast_fusion), kind=kLoop, calls=%fused_computation.11 | loop fusion | flops 9830400 | bytes 32768000 | tf_op jit(solution)/shard_map/mul | solution.py:62
  349.4 10.9 %fusion.5 = bf16[1,32,320,320]{2,3,1,0:T(8,128)(2,1)S(1)} fusion(f32[32,2,2,320,320]{3,4,1,2,0:T(8,128)} %convolution_bitcast_fusion), kind=kLoop, calls=%fused_computation.10 | loop fusion | flops 9830400 | bytes 32768000 | tf_op jit(solution)/shard_map/mul | solution.py:61
  360.3 7.5 %pad_maximum_fusion = bf16[2,32,320,320]{2,3,1,0:T(8,128)(2,1)} fusion(bf16[1,32,320,320]{2,3,1,0:T(8,128)(2,1)S(1)} %fusion.6, bf16[1,32,320,320]{2,3,1,0:T(8,128)(2,1)S(1)} %fusion.5), kind=kLoop, calls=%fused_computation.9 | loop fusion | flops 6553600 | bytes 26214400 | tf_op jit(solution)/shard_map/stack | solution.py:63
  367.8 0.0 copy-start.1
  367.8 21.1 %copy.27 = bf16[2,32,320,320]{3,2,1,0:T(8,128)(2,1)} copy(bf16[2,32,320,320]{2,3,1,0:T(8,128)(2,1)} %pad_maximum_fusion) | data formatting | bytes 26214400 | tf_op jit(solution)/shard_map/stack | solution.py:63
  388.8 0.0 copy-done.1
  (3 shorter events, 0.1 us)
Async XLA Ops:
  6.5 3.2 copy-start
  6.5 286.2 %all-gather.2.cloned.1.call-start = ((), (), s32[]{:S(2)}) async-start(), calls=%async_computation.1 | async-start | bytes 44564480 | tf_op jit(solution)/shard_map/all_gather | solution.py:45
  9.7 1.5 copy-start.2
  367.8 21.1 %copy-start.1 = (bf16[80,28,512]{2,0,1:T(8,128)(2,1)S(1)}, bf16[80,28,512]{2,0,1:T(8,128)(2,1)}, u32[]{:S(2)}) copy-start(bf16[80,28,512]{2,0,1:T(8,128)(2,1)} %param.2) | copy-start | bytes 6881284
Sparse Core Ops, SparseCore 0:
  83.5 209.1 all-gather.1
